TPU v7x, 256 devices: a whole 4x4x8 slice. The times are simulated.
256 devices in a mesh: seq: 64 (over y, z_lo, x), tensor: 4 (over z_hi, core).
Axes of the slice: x: 4, y: 4, z: 8 (z_hi: 2, z_lo: 4; z = z_hi * 4 + z_lo), core: 2. Of those that a mesh axis runs over, the one named last changes fastest.
Arguments:
- queries: bfloat16 [32768, 3072], P('seq', 'tensor'), may hold values from -180 to 180, as said below
- ref_keys: bfloat16 [1024, 3072], P('seq', 'tensor'), may hold values from -6 to 6
- ref_values: bfloat16 [1024, 3072], P('seq', 'tensor'), may hold values from -6 to 6
- grad_out: bfloat16 [32768, 3072], P('seq', 'tensor'), may hold values from -12 to 12
- key_weight: bfloat16 [3072, 3072], P(None, 'tensor'), may hold values from -0.109375 to 0.109375
- value_weight: bfloat16 [3072, 3072], P(None, 'tensor'), may hold values from -0.109375 to 0.109375
Outputs:
- grad_queries: bfloat16 [32768, 3072], P('seq', 'tensor')
- grad_ref_rows: bfloat16 [1024, 3072], P('seq', 'tensor')
Inputs may be any that keep to these rules, and one draw needn't show every extreme that they name: `queries`: queries of order one, some rows larger.
All inputs are finite; a program needn't handle non-finite values.
Results may differ from a plain program's by a relative error of at most 0.015.
Values may be sent and summed in bfloat16 or wider, within the bound.
No kernel may reach another device: no remote copies, remote signals or barrier semaphores. Data moves between devices by JAX's collectives and lax.ppermute only.
A program may use at most 128 MiB of HBM per device.

v0:
```python
import jax
import jax.numpy as jnp
from jax import lax
from jax.sharding import PartitionSpec as P

HD = 128


def head_terms(queries, keys_all, values_all, grad_out, head):
    scale = 1.0 / HD**0.5
    lo_col = head * HD
    query_h = queries[:, lo_col : lo_col + HD]
    key_h = keys_all[:, lo_col : lo_col + HD]
    value_h = values_all[:, lo_col : lo_col + HD]
    grad_h = grad_out[:, lo_col : lo_col + HD]
    scores = jnp.dot(query_h, key_h.T, preferred_element_type=jnp.float32) * scale
    probs = jax.nn.softmax(scores, axis=-1)
    probs_b = probs.astype(jnp.bfloat16)
    grad_probs = jnp.dot(grad_h, value_h.T, preferred_element_type=jnp.float32)
    delta = jnp.sum(probs * grad_probs, axis=-1, keepdims=True)
    grad_scores = (probs * (grad_probs - delta)).astype(jnp.bfloat16)
    grad_query = (jnp.dot(grad_scores, key_h, preferred_element_type=jnp.float32) * scale).astype(
        jnp.bfloat16
    )
    grad_key = jnp.dot(grad_scores.T, query_h, preferred_element_type=jnp.float32) * scale
    grad_value = jnp.dot(probs_b.T, grad_h, preferred_element_type=jnp.float32)
    return (grad_query, grad_key, grad_value)


def head_range(queries, keys_all, values_all, grad_out, first, count):
    query_list, key_list, value_list = ([], [], [])
    for head in range(first, first + count):
        grad_query, grad_key, grad_value = head_terms(queries, keys_all, values_all, grad_out, head)
        query_list.append(grad_query)
        key_list.append(grad_key)
        value_list.append(grad_value)
    return (query_list, jnp.concatenate(key_list, axis=1), jnp.concatenate(value_list, axis=1))


def project_exact(keys_own, values_own, key_weight, value_weight):
    key_cols = key_weight.astype(jnp.float32)
    value_cols = value_weight.astype(jnp.float32)
    rows = jnp.dot(
        keys_own, key_cols.T, precision=lax.Precision.HIGHEST, preferred_element_type=jnp.float32
    )
    return rows + jnp.dot(
        values_own,
        value_cols.T,
        precision=lax.Precision.HIGHEST,
        preferred_element_type=jnp.float32,
    )


def shards(queries, ref_keys, ref_values, grad_out, key_weight, value_weight):
    keys_all, values_all = (
        lax.all_gather(ref_keys, "seq", axis=0, tiled=True),
        lax.all_gather(ref_values, "seq", axis=0, tiled=True),
    )
    local_heads = queries.shape[1] // HD
    ranges = (0, local_heads)
    query_list = []
    first, count = ranges
    group_queries, key_terms, value_terms = head_range(
        queries, keys_all, values_all, grad_out, first, count
    )
    query_list = query_list + group_queries
    key_part = key_terms.astype(jnp.bfloat16)
    value_part = value_terms.astype(jnp.bfloat16)
    key_held, value_held = lax.optimization_barrier((key_part, value_part))
    key_wide = key_held.astype(jnp.float32)
    value_wide = value_held.astype(jnp.float32)
    keys_own = lax.psum_scatter(key_wide, "seq", scatter_dimension=0, tiled=True)
    values_own = lax.psum_scatter(value_wide, "seq", scatter_dimension=0, tiled=True)
    partial_value = project_exact(keys_own, values_own, key_weight, value_weight)
    grad_queries = jnp.concatenate(query_list, axis=1)
    grad_rows = lax.psum_scatter(
        partial_value.astype(jnp.bfloat16), "tensor", scatter_dimension=1, tiled=True
    )
    return (grad_queries, grad_rows)


def solution(mesh):
    placed = (
        P("seq", "tensor"),
        P("seq", "tensor"),
        P("seq", "tensor"),
        P("seq", "tensor"),
        P(None, "tensor"),
        P(None, "tensor"),
    )
    return jax.shard_map(
        shards,
        mesh=mesh,
        in_specs=placed,
        out_specs=(P("seq", "tensor"), P("seq", "tensor")),
        check_vma=False,
    )
```

profile of v0, /device:TPU:1, one launch (start us, length us, event | category | flops | bytes accessed | tf_op | source)
XLA Modules:
  0.0 1526.0 jit_solution(15675450137437767035)
XLA Ops:
  7.2 0.7 all-gather.3.cloned.1.call-update
  7.9 0.7 all-gather.5.cloned.1.call-update
  8.7 308.8 %all-gather.3.cloned.1.call-done = bf16[1024,768]{1,0:T(8,128)(2,1)} async-done(((bf16[16,768]{1,0:T(8,128)(2,1)}), bf16[1024,768]{1,0:T(8,128)(2,1)}) %all-gather.3.cloned.1.call-update) | async-done | bytes 1572880 | tf_op jit(solution)/shard_map/all_gather | solution.py:56
  317.5 1.5 multiply_reduce_fusion.11
  319.0 0.5 fusion.2
  319.5 2.3 fusion.25
  321.8 344.2 %all-gather.5.cloned.1.call-done = bf16[1024,768]{1,0:T(8,128)(2,1)} async-done(((bf16[16,768]{1,0:T(8,128)(2,1)}), bf16[1024,768]{1,0:T(8,128)(2,1)}) %all-gather.5.cloned.1.call-update) | async-done | bytes 1572880 | tf_op jit(solution)/shard_map/all_gather | solution.py:57
  666.0 1.7 multiply_reduce_fusion.5
  667.7 0.6 multiply_convert_fusion.5
  668.3 0.5 copy-done.14
  668.8 0.4 fusion.14
  669.2 0.2 copy-done
  669.4 0.5 multiply_reduce_fusion.10
  669.9 0.5 fusion.4
  670.4 0.4 copy-done.11
  670.8 0.2 copy-done.16
  671.0 0.7 fusion.26
  671.7 0.5 multiply_reduce_fusion.9
  672.2 0.5 fusion.6
  672.7 0.7 fusion.27
  673.4 0.5 multiply_reduce_fusion.8
  673.9 0.5 fusion.8
  674.4 0.7 fusion.28
  675.1 0.5 multiply_reduce_fusion.7
  675.6 0.5 fusion.10
  676.2 0.7 fusion.29
  676.9 0.5 multiply_reduce_fusion.6
  677.4 0.5 fusion.12
  677.9 0.7 fusion.30
  678.6 0.7 copy-done.15
  679.3 0.7 multiply_reduce_fusion.4
  680.0 0.4 copy-done.12
  680.5 0.6 multiply_convert_fusion.4
  681.1 0.5 fusion.16
  681.6 0.7 multiply_reduce_fusion.3
  682.3 0.6 multiply_convert_fusion.3
  683.0 0.3 fusion.18
  683.3 0.7 multiply_reduce_fusion.2
  684.0 0.6 multiply_convert_fusion.2
  684.7 0.3 fusion.20
  685.0 0.7 multiply_reduce_fusion.1
  685.8 0.6 multiply_convert_fusion.1
  686.4 0.3 fusion.22
  686.7 0.7 multiply_reduce_fusion
  687.5 0.6 multiply_convert_fusion
  688.1 1.1 copy-done.5
  689.2 0.3 fusion.24
  689.5 2.1 copy.10
  691.7 1.3 copy-done.13
  693.0 2.1 copy.12
  695.1 0.3 reduce-scatter.8.cloned.1.call-start
  695.4 1.1 copy-done.1
  696.5 0.5 fusion.32
  697.0 1.9 fusion.34
  698.9 0.5 fusion.36
  699.4 0.5 fusion.38
  699.9 0.5 fusion.40
  700.3 361.1 %reduce-scatter.10.cloned.1.call-done = f32[16,768]{1,0:T(8,128)} async-done(((f32[1024,768]{1,0:T(8,128)}), f32[16,768]{1,0:T(8,128)}) %reduce-scatter.10.cloned.1.call-update) | async-done | bytes 49168
  1061.5 6.8 fusion.109
  1068.3 366.2 %reduce-scatter.12.cloned.1.call-done = f32[16,768]{1,0:T(8,128)} async-done(((f32[1024,768]{1,0:T(8,128)}), f32[16,768]{1,0:T(8,128)}) %reduce-scatter.12.cloned.1.call-update) | async-done | bytes 49168
  1434.5 6.7 fusion
  1441.3 0.5 fusion.42
  1441.8 1.2 copy.9
  1442.9 76.6 %reduce-scatter.8.cloned.1.call-done = bf16[16,768]{1,0:T(8,128)(2,1)} async-done(((bf16[16,3072]{1,0:T(8,128)(2,1)}), bf16[16,768]{1,0:T(8,128)(2,1)}) %reduce-scatter.8.cloned.1.call-update) | async-done | bytes 24592 | tf_op jit(solution)/shard_map/reduce_scatter | solution.py:76
  (32 shorter events, 0.3 us)
Async XLA Ops:
  7.2 310.3 %all-gather.3.cloned.1.call-start = ((), (), s32[]{:S(2)}) async-start(), calls=%async_computation.3 | async-start | bytes 1597440 | tf_op jit(solution)/shard_map/all_gather | solution.py:56
  7.9 658.1 %all-gather.5.cloned.1.call-start = ((), (), s32[]{:S(2)}) async-start(), calls=%async_computation.4 | async-start | bytes 1597440 | tf_op jit(solution)/shard_map/all_gather | solution.py:57
  8.6 1052.8 %reduce-scatter.10.cloned.1.call-start = ((), (), s32[]{:S(2)}) async-start(), calls=%async_computation.6 | async-start | bytes 3194880
  667.7 1.1 copy-start.14
  667.7 1.7 copy-start
  669.4 1.4 copy-start.11
  669.4 1.6 copy-start.16
  677.9 1.4 copy-start.15
  679.3 1.1 copy-start.12
  681.1 1.3 copy-start.2
  683.0 1.1 copy-start.3
  684.7 1.1 copy-start.7
  686.4 1.1 copy-start.9
  688.1 1.1 copy-start.5
  691.6 1.4 copy-start.13
  691.6 742.9 %reduce-scatter.12.cloned.1.call-start = ((), (), s32[]{:S(2)}) async-start(), calls=%async_computation.7 | async-start | bytes 3194880
  695.1 1.4 copy-start.1
  695.1 824.4 %reduce-scatter.8.cloned.1.call-start = ((), (), s32[]{:S(2)}) async-start(), calls=%async_computation.5 | async-start | bytes 122880 | tf_op jit(solution)/shard_map/reduce_scatter | solution.py:76
  696.5 2.4 copy-start.4
  696.5 2.9 copy-start.8
  697.0 2.9 copy-start.10
  1068.3 373.0 %copy-start.6 = (bf16[512,1024]{1,0:T(8,128)(2,1)S(1)}, bf16[512,1024]{1,0:T(8,128)(2,1)}, u32[]{:S(2)}) copy-start(bf16[512,1024]{1,0:T(8,128)(2,1)} %copy-done.5) | copy-start | bytes 3145732
Sparse Core Ops, SparseCore 0:
  9.8 307.6 all-gather.2
  319.3 346.6 all-gather.4
  691.7 369.6 reduce-scatter.9
  1064.0 370.4 reduce-scatter.11
  1441.4 78.0 reduce-scatter.7
where the time goes:
time: 1530 us
  waiting for transfers between devices  1460 us (95%)
  matrix products  35.2 us (2%)
    unnamed x7, waiting for transfers between devices  729 us
    all_gather x1, waiting for transfers between devices, shards(): lax.all_gather(ref_values, 'seq', axis=0, tiled=True)  344 us
    all_gather x1, waiting for transfers between devices, shards(): lax.all_gather(ref_keys, 'seq', axis=0, tiled=True)  309 us
    reduce_scatter x1, waiting for transfers between devices, shards(): lax.psum_scatter(partial_value.astype(jnp.bfloat16), 'tensor', scatter_di...  76.6 us
  transfers between devices with their start and end apart: 5, of which 5 were waited for; matrix products, arithmetic and copies ran while one was open for 1% of the time, Pallas kernels for 0%

commit v1 on v0

--- a/solution.py
+++ b/solution.py
@@ -52,8 +52,11 @@
 
 
 def shards(queries, ref_keys, ref_values, grad_out, key_weight, value_weight):
+    supply_all_tasks_in = lambda patch: jnp.concatenate(
+        lax.all_to_all(jnp.stack([patch for _ in range(lax.axis_size("seq"))]), "seq", 0, 0), axis=0
+    )
     keys_all, values_all = (
-        lax.all_gather(ref_keys, "seq", axis=0, tiled=True),
+        supply_all_tasks_in(ref_keys),
         lax.all_gather(ref_values, "seq", axis=0, tiled=True),
     )
     local_heads = queries.shape[1] // HD

time: 1530 us -> 1200 us (0.78)
  waiting for transfers between devices: 1460 us -> 1100 us
    all_gather x1 -> x0, waiting for transfers between devices: 309 us -> none  [shards(): lax.all_gather(ref_keys, 'seq', axis=0, tiled=True)]
    all_gather x1, waiting for transfers between devices: 344 us -> 257 us  [shards(): lax.all_gather(ref_values, 'seq', axis=0, tiled=True)]
    all_to_all x0 -> x1, waiting for transfers between devices: none -> 38.2 us  [shards(): lax.all_to_all(jnp.stack([patch for _ in range(lax.axis_size('seq'))]), '...]
    unnamed x7 -> x6, waiting for transfers between devices: 729 us -> 726 us
  transfers between devices with their start and end apart: 5 -> 5, of which waited for: 5 -> 5; matrix products, arithmetic and copies ran while one was open for 1% -> 3% of each run, Pallas kernels for 0% -> 0%
where the time goes in v1:
time: 1200 us
  waiting for transfers between devices  1100 us (92%)
  matrix products  48.4 us (4%)
  local copies, waits for them, and re-layouts  17.7 us (1%)
  between operations  14 us (1%)
  starting transfers between devices  12.9 us (1%)
    unnamed x6, waiting for transfers between devices  726 us
    all_gather x1, waiting for transfers between devices, shards(): lax.all_gather(ref_values, 'seq', axis=0, tiled=True)  257 us
    reduce_scatter x1, waiting for transfers between devices, shards(): lax.psum_scatter(partial_value.astype(jnp.bfloat16), 'tensor', scatter_di...  74.5 us
    all_to_all x1, waiting for transfers between devices, shards(): lax.all_to_all(jnp.stack([patch for _ in range(lax.axis_size('seq'))]), '...  38.2 us
  transfers between devices with their start and end apart: 5, of which 5 were waited for; matrix products, arithmetic and copies ran while one was open for 3% of the time, Pallas kernels for 0%

profile of v1, /device:TPU:1, one launch (start us, length us, event | category | flops | bytes accessed | tf_op | source)
XLA Modules:
  0.0 1195.8 jit_solution(5844839014325143556)
XLA Ops:
  7.2 2.1 stack.2
  9.2 12.6 %all-to-all-start = ((bf16[64,16,768]{2,1,0:T(8,128)(2,1)}), bf16[64,16,768]{2,1,0:T(8,128)(2,1)S(1)}, u32[]{:S(2)}, u32[]{:S(2)}) async-start(bf16[64,16,768]{2,1,0:T(8,128)(2,1)} %stack.2), calls=%async_computation | async-start | bytes 3145728 | tf_op jit(solution)/shard_map/all_to_all | solution.py:56
  21.8 0.7 all-gather.2.cloned.1.call-update
  22.6 38.2 %all-to-all-done = bf16[64,16,768]{2,1,0:T(8,128)(2,1)S(1)} async-done(((bf16[64,16,768]{2,1,0:T(8,128)(2,1)}), bf16[64,16,768]{2,1,0:T(8,128)(2,1)S(1)}, u32[]{:S(2)}, u32[]{:S(2)}) %all-to-all-start) | async-done | bytes 1572896 | tf_op jit(solution)/shard_map/all_to_all | solution.py:56
  60.7 0.5 multiply_reduce_fusion.11
  61.3 0.5 fusion.2
  61.8 1.8 multiply_reduce_fusion.10
  63.6 1.8 multiply_reduce_fusion.9
  65.4 1.7 multiply_reduce_fusion.8
  67.1 1.8 multiply_reduce_fusion.7
  68.9 1.5 multiply_reduce_fusion.6
  70.3 2.3 fusion.25
  72.6 256.9 %all-gather.2.cloned.1.call-done = bf16[1024,768]{1,0:T(8,128)(2,1)} async-done(((bf16[16,768]{1,0:T(8,128)(2,1)}), bf16[1024,768]{1,0:T(8,128)(2,1)}) %all-gather.2.cloned.1.call-update) | async-done | bytes 1572880 | tf_op jit(solution)/shard_map/all_gather | solution.py:60
  329.5 2.6 multiply_reduce_fusion.5
  332.1 0.6 multiply_convert_fusion.5
  332.7 0.5 copy-done.21
  333.2 1.1 fusion.14
  334.3 0.5 fusion.4
  335.1 0.7 fusion.26
  335.8 0.9 copy-done.2
  336.7 0.5 fusion.6
  337.2 0.7 fusion.27
  337.9 0.9 copy-done.1
  338.8 0.5 fusion.8
  339.3 0.7 fusion.28
  340.0 0.9 copy-done
  340.9 0.5 fusion.10
  341.5 0.7 fusion.29
  342.1 0.5 fusion.12
  342.7 0.7 fusion.30
  343.3 0.7 copy-done.22
  344.1 0.7 multiply_reduce_fusion.4
  344.8 0.4 copy-done.18
  345.2 0.8 multiply_convert_fusion.4
  346.0 1.1 fusion.16
  347.1 0.7 multiply_reduce_fusion.3
  347.8 0.6 multiply_convert_fusion.3
  348.4 1.1 fusion.18
  349.5 0.7 multiply_reduce_fusion.2
  350.2 0.6 multiply_convert_fusion.2
  350.9 1.1 fusion.20
  351.9 0.7 multiply_reduce_fusion.1
  352.7 0.6 multiply_convert_fusion.1
  353.3 1.1 fusion.22
  354.4 0.7 multiply_reduce_fusion
  355.1 0.6 multiply_convert_fusion
  355.7 1.0 copy-done.11
  356.7 1.1 fusion.24
  357.8 3.1 copy.10
  361.0 1.3 copy-done.19
  362.3 2.1 copy.12
  364.7 1.1 copy-done.7
  365.8 1.1 fusion.32
  366.9 2.4 fusion.34
  369.4 1.1 fusion.36
  370.5 1.1 fusion.38
  371.6 1.1 fusion.40
  372.8 357.7 %reduce-scatter.10.cloned.1.call-done = f32[16,768]{1,0:T(8,128)} async-done(((f32[1024,768]{1,0:T(8,128)}), f32[16,768]{1,0:T(8,128)}) %reduce-scatter.10.cloned.1.call-update) | async-done | bytes 49168
  730.5 6.1 fusion.109
  736.6 368.0 %reduce-scatter.12.cloned.1.call-done = f32[16,768]{1,0:T(8,128)} async-done(((f32[1024,768]{1,0:T(8,128)}), f32[16,768]{1,0:T(8,128)}) %reduce-scatter.12.cloned.1.call-update) | async-done | bytes 49168
  1104.6 6.8 fusion
  1111.4 1.1 fusion.42
  1112.5 2.3 copy.9
  1114.8 74.5 %reduce-scatter.8.cloned.1.call-done = bf16[16,768]{1,0:T(8,128)(2,1)} async-done(((bf16[16,3072]{1,0:T(8,128)(2,1)}), bf16[16,768]{1,0:T(8,128)(2,1)}) %reduce-scatter.8.cloned.1.call-update) | async-done | bytes 24592 | tf_op jit(solution)/shard_map/reduce_scatter | solution.py:79
  (46 shorter events, 0.8 us)
Async XLA Ops:
  7.2 53.6 %copy-start.20 = (bf16[512,768]{1,0:T(8,128)(2,1)S(1)}, bf16[512,768]{1,0:T(8,128)(2,1)}, u32[]{:S(2)}) copy-start(bf16[512,768]{1,0:T(8,128)(2,1)} %param.6) | copy-start | bytes 2359300
  9.2 51.5 %all-to-all-start = ((bf16[64,16,768]{2,1,0:T(8,128)(2,1)}), bf16[64,16,768]{2,1,0:T(8,128)(2,1)S(1)}, u32[]{:S(2)}, u32[]{:S(2)}) async-start(bf16[64,16,768]{2,1,0:T(8,128)(2,1)} %stack.2), calls=%async_computation | async-start | bytes 3145728 | tf_op jit(solution)/shard_map/all_to_all | solution.py:56
  21.8 307.7 %all-gather.2.cloned.1.call-start = ((), (), s32[]{:S(2)}) async-start(), calls=%async_computation.4 | async-start | bytes 1597440 | tf_op jit(solution)/shard_map/all_gather | solution.py:60
  22.5 708.0 %reduce-scatter.10.cloned.1.call-start = ((), (), s32[]{:S(2)}) async-start(), calls=%async_computation.6 | async-start | bytes 3194880
  60.7 6.4 copy-start.6
  61.3 9.1 copy-start.4
  329.5 2.6 copy-start.5
  332.1 1.1 copy-start.21
  332.1 2.2 copy-start.3
  333.2 1.7 copy-start.17
  333.2 1.9 copy-start.23
  335.1 1.6 copy-start.2
  337.2 1.6 copy-start.1
  339.3 1.6 copy-start
  342.7 1.4 copy-start.22
  344.1 1.1 copy-start.18
  346.0 1.8 copy-start.8
  348.4 1.8 copy-start.9
  350.8 1.8 copy-start.13
  353.3 1.8 copy-start.15
  355.7 1.0 copy-start.11
  360.9 1.4 copy-start.19
  360.9 743.7 %reduce-scatter.12.cloned.1.call-start = ((), (), s32[]{:S(2)}) async-start(), calls=%async_computation.7 | async-start | bytes 3194880
  364.4 1.4 copy-start.7
  364.4 824.9 %reduce-scatter.8.cloned.1.call-start = ((), (), s32[]{:S(2)}) async-start(), calls=%async_computation.5 | async-start | bytes 122880 | tf_op jit(solution)/shard_map/reduce_scatter | solution.py:79
  365.8 3.6 copy-start.10
  365.8 4.7 copy-start.14
  366.9 4.7 copy-start.16
  736.6 374.8 %copy-start.12 = (bf16[512,1024]{1,0:T(8,128)(2,1)S(1)}, bf16[512,1024]{1,0:T(8,128)(2,1)}, u32[]{:S(2)}) copy-start(bf16[512,1024]{1,0:T(8,128)(2,1)} %copy-done.11) | copy-start | bytes 3145732
Sparse Core Ops, SparseCore 0:
  24.4 305.0 all-gather.1
  361.0 369.4 reduce-scatter.9
  733.2 371.3 reduce-scatter.11
  1111.5 77.7 reduce-scatter.7
